TPU v7x, 512 devices: a whole 4x8x8 slice. The times are simulated.
512 devices in a mesh: row: 32 (over z, x), col: 16 (over y, core).
Axes of the slice: x: 4, y: 8, z: 8, core: 2. Of those that a mesh axis runs over, the one named last changes fastest.
Arguments:
- density: float32 [32, 256, 2048], P(None, 'row', 'col'), may hold values from 0 to 1
- threshold_index: int32 [3], replicated, may hold values from 4 to 12
- channel_width: int32 [30], replicated, may hold values from 0 to 9
- sigma_table: float32 [10], replicated, may hold values from 1.5 to 64
Outputs:
- compliance: float32 [30], replicated
- sensitivity: float32 [32, 256, 2048], P(None, 'row', 'col')
All inputs are finite; a program needn't handle non-finite values.
Results may differ from a plain program's by a relative error of at most 0.0013.
Values may be sent and summed in bfloat16 or wider, within the bound.
No kernel may reach another device: no remote copies, remote signals or barrier semaphores. Data moves between devices by JAX's collectives and lax.ppermute only.
A program may use at most 64 MiB of HBM per device.

v0:
```python
from functools import partial
import jax
import jax.numpy as jnp
from jax import lax
from jax.sharding import PartitionSpec as P

VARIANTS = 3
WIDTHS = 10
CHANNELS = 30
HALF = 128
sharpness = 8.0
spread_floor = 0.0001


def extended(x, sides, width):
    for axis, dim in sides:
        size, length = (lax.axis_size(axis), x.shape[dim])
        up = [(i, (i + 1) % size) for i in range(size - 1)]
        down = [(j, i) for i, j in up]
        last = lax.slice_in_dim(x, length - width, length, axis=dim)
        first = lax.slice_in_dim(x, 0, width, axis=dim)
        before = lax.ppermute(last, axis, up)
        after = lax.ppermute(first, axis, down)
        x = jnp.concatenate([before, x, after], axis=dim)
    return x


def project(density, threshold_index):
    levels = threshold_index.astype(jnp.float32) / 16.0
    levels = levels.reshape((-1,) + (1,) * density.ndim)
    low = jnp.tanh(sharpness * levels)
    high = jnp.tanh(sharpness * (1.0 - levels))
    return (low + jnp.tanh(sharpness * (density - levels))) / (low + high)


def slope(density, threshold_index):
    levels = threshold_index.astype(jnp.float32) / 16.0
    levels = levels.reshape((-1,) + (1,) * density.ndim)
    low = jnp.tanh(sharpness * levels)
    high = jnp.tanh(sharpness * (1.0 - levels))
    inner = jnp.tanh(sharpness * (density - levels))
    return sharpness * (1.0 - inner * inner) / (low + high)


def gauss_band(width_value, num_rows, num_cols, offset):
    row_ids = lax.broadcasted_iota(jnp.float32, (num_rows, num_cols), 0)
    col_ids = lax.broadcasted_iota(jnp.float32, (num_rows, num_cols), 1)
    offsets = row_ids - col_ids - offset
    tap_axis = jnp.arange(-HALF, HALF + 1).astype(jnp.float32)
    inverse = 1.0 / jnp.sum(jnp.exp(-tap_axis * tap_axis / (2.0 * width_value * width_value)))
    values = jnp.exp(-offsets * offsets / (2.0 * width_value * width_value)) * inverse
    return jnp.where(jnp.abs(offsets) <= HALF, values, 0.0).astype(jnp.bfloat16)


def width_of(sigma_table, channel_width, index):
    slot = jnp.sum(jnp.where(jnp.arange(channel_width.shape[0]) == index, channel_width, 0))
    return jnp.sum(jnp.where(jnp.arange(sigma_table.shape[0]) == slot, sigma_table, 0.0))


def along_x(sigma_table, channel_width, wide, index):
    variant = index // WIDTHS
    cols_out = wide.shape[-1] - 2 * HALF
    matrix = gauss_band(
        width_of(sigma_table, channel_width, index), wide.shape[-1], cols_out, float(HALF)
    )
    source = lax.dynamic_index_in_dim(wide, variant, 0, keepdims=False)
    return jnp.einsum("...j,ji->...i", source, matrix, preferred_element_type=jnp.float32).astype(
        jnp.bfloat16
    )


def per_device(density, threshold_index, channel_width, sigma_table):
    channel_ids = jnp.arange(CHANNELS, dtype=jnp.int32)
    smooth_x = partial(along_x, sigma_table, channel_width)
    wide_density = extended(density, (("col", 2),), HALF)
    wide = project(wide_density, threshold_index).astype(jnp.bfloat16)
    panels = lax.map(partial(smooth_x, wide), channel_ids)
    middle = wide[..., HALF : wide.shape[-1] - HALF]
    panels, variants = (
        lax.all_to_all(panels, "row", split_axis=1, concat_axis=2, tiled=True),
        lax.all_to_all(middle, "row", split_axis=1, concat_axis=2, tiled=True),
    )
    length = variants.shape[2]

    def along_y(index):
        variant = index // WIDTHS
        matrix = gauss_band(width_of(sigma_table, channel_width, index), length, length, 0.0)
        source = lax.dynamic_index_in_dim(panels, index, 0, keepdims=False)
        field = jnp.einsum("zyx,yw->zwx", source, matrix, preferred_element_type=jnp.float32)
        owner = lax.dynamic_index_in_dim(variants, variant, 0, keepdims=False).astype(jnp.float32)
        return (field, jnp.sum(owner * field))

    smoothed, partials = lax.map(along_y, channel_ids)
    cell_count = (
        lax.axis_size("row") * lax.axis_size("col") * variants.shape[1] * length * variants.shape[3]
    )
    compliance = lax.psum(partials, ("row", "col")) / cell_count
    mean_value = jnp.mean(compliance)
    spread = jnp.sqrt(jnp.mean((compliance - mean_value) ** 2) + spread_floor)
    weights = (1.0 + (compliance - mean_value) / spread) / CHANNELS
    member = (
        lax.broadcasted_iota(jnp.int32, (VARIANTS, CHANNELS), 1) // WIDTHS
        == lax.broadcasted_iota(jnp.int32, (VARIANTS, CHANNELS), 0)
    ).astype(jnp.float32)
    combined = jnp.einsum(
        "vc,czyx->vzyx",
        member * (2.0 * weights)[None, :],
        smoothed,
        precision=lax.Precision.HIGHEST,
    )
    returned = lax.all_to_all(combined, "row", split_axis=2, concat_axis=1, tiled=True)
    sensitivity = jnp.sum(slope(density, threshold_index) * returned, axis=0)
    return (compliance, sensitivity)


def solution(mesh):
    in_specs = (P(None, "row", "col"), P(), P(), P())
    out_specs = (P(), P(None, "row", "col"))
    return jax.shard_map(
        per_device, mesh=mesh, in_specs=in_specs, out_specs=out_specs, check_vma=False
    )
```

profile of v0, /device:TPU:16, one launch (start us, length us, event | category | flops | bytes accessed | tf_op | source)
XLA Modules:
  0.0 859.1 jit_solution(10198214440540660656)
XLA Ops:
  0.6 2.1 collective-permute-start
  2.7 3.6 collective-permute-start.1
  7.3 1.9 collective-permute-done.1
  11.1 13.2 %all-to-all-start.1 = ((bf16[3,32,8,128]{3,2,0,1:T(8,128)(2,1)}), bf16[3,32,8,128]{3,2,0,1:T(8,128)(2,1)S(1)}, u32[]{:S(2)}, u32[]{:S(2)}) async-start(bf16[3,32,8,128]{3,2,0,1:T(8,128)(2,1)} %slice.4), calls=%async_computation.1 | async-start | bytes 393216 | tf_op jit(solution)/shard_map/all_to_all | solution.py:81
  24.3 259.6 %while.26 = (s32[]{:T(128)}, bf16[30,32,8,128]{3,2,0,1:T(8,128)(2,1)}, s32[30]{0:T(128)S(1)}, bf16[3,32,8,384]{3,2,0,1:T(8,128)(2,1)S(1)}, s32[30]{0:T(128)S(1)}...) while((s32[]{:T(128)}, ...), condition=%wide.region_4.5_spmd, body=%wide.region_0.4_spmd.sunk | while | flops 25691788 | bytes 263137 | solution.py:77
  283.9 9.8 %all-to-all-start = ((bf16[30,32,8,128]{3,2,0,1:T(8,128)(2,1)}), bf16[30,32,8,128]{3,2,0,1:T(8,128)(2,1)S(1)}, u32[]{:S(2)}, u32[]{:S(2)}) async-start(bf16[30,32,8,128]{3,2,0,1:T(8,128)(2,1)} %get-tuple-element.184), calls=%async_computation | async-start | bytes 3932160 | tf_op jit(solution)/shard_map/all_to_all | solution.py:80
  293.8 48.5 %all-to-all-done = bf16[30,32,8,128]{3,2,0,1:T(8,128)(2,1)S(1)} async-done(((bf16[30,32,8,128]{3,2,0,1:T(8,128)(2,1)}), bf16[30,32,8,128]{3,2,0,1:T(8,128)(2,1)S(1)}, u32[]{:S(2)}, u32[]{:S(2)}) %all-to-all-start) | async-done | bytes 1966112 | tf_op jit(solution)/shard_map/all_to_all | solution.py:80
  342.3 1.8 copy.40
  344.2 388.2 %while.27 = (s32[]{:T(128)}, f32[30,1,256,128]{3,2,1,0:T(8,128)}, f32[30]{0:T(128)S(1)}, s32[30]{0:T(128)S(1)}, s32[30]{0:T(128)S(1)}, /*index=5*/f32[10]{0:T(12...) while((s32[]{:T(128)}, f32[30,1,256,128]{3,2,1,0:T(8,128)}, ...), condition=%wide.region_10.11_spmd, body=%wide.region_5.10_spmd.sunk | while | flops 17467012 | bytes 525359 | solution.py:93
  346.7 1.4 fusion.78
  351.9 1.8 bitcast_dynamic-update-slice_fusion.2
  359.6 1.4 fusion.78
  364.9 1.8 bitcast_dynamic-update-slice_fusion.2
  372.6 1.4 fusion.78
  377.8 1.8 bitcast_dynamic-update-slice_fusion.2
  385.5 1.4 fusion.78
  390.8 1.8 bitcast_dynamic-update-slice_fusion.2
  398.5 1.4 fusion.78
  403.7 1.8 bitcast_dynamic-update-slice_fusion.2
  411.4 1.4 fusion.78
  416.6 1.8 bitcast_dynamic-update-slice_fusion.2
  424.3 1.4 fusion.78
  429.6 1.8 bitcast_dynamic-update-slice_fusion.2
  437.3 1.4 fusion.78
  442.5 1.8 bitcast_dynamic-update-slice_fusion.2
  450.2 1.4 fusion.78
  455.5 1.8 bitcast_dynamic-update-slice_fusion.2
  468.4 1.8 bitcast_dynamic-update-slice_fusion.2
  476.1 1.4 fusion.78
  481.4 1.8 bitcast_dynamic-update-slice_fusion.2
  489.1 1.4 fusion.78
  494.3 1.8 bitcast_dynamic-update-slice_fusion.2
  502.0 1.4 fusion.78
  507.2 1.8 bitcast_dynamic-update-slice_fusion.2
  514.9 1.4 fusion.78
  520.2 1.8 bitcast_dynamic-update-slice_fusion.2
  533.1 1.8 bitcast_dynamic-update-slice_fusion.2
  546.0 1.8 bitcast_dynamic-update-slice_fusion.2
  553.8 1.4 fusion.78
  559.0 1.8 bitcast_dynamic-update-slice_fusion.2
  571.9 1.8 bitcast_dynamic-update-slice_fusion.2
  579.6 1.4 fusion.78
  584.9 1.8 bitcast_dynamic-update-slice_fusion.2
  597.8 1.8 bitcast_dynamic-update-slice_fusion.2
  610.8 1.8 bitcast_dynamic-update-slice_fusion.2
  623.7 1.8 bitcast_dynamic-update-slice_fusion.2
  636.6 1.8 bitcast_dynamic-update-slice_fusion.2
  644.3 1.4 fusion.78
  649.6 1.8 bitcast_dynamic-update-slice_fusion.2
  657.3 1.4 fusion.78
  662.5 1.8 bitcast_dynamic-update-slice_fusion.2
  670.2 1.4 fusion.78
  675.5 1.8 bitcast_dynamic-update-slice_fusion.2
  683.2 1.4 fusion.78
  688.4 1.8 bitcast_dynamic-update-slice_fusion.2
  696.1 1.4 fusion.78
  701.4 1.8 bitcast_dynamic-update-slice_fusion.2
  709.1 1.4 fusion.78
  714.3 1.8 bitcast_dynamic-update-slice_fusion.2
  722.0 1.4 fusion.78
  727.2 1.8 bitcast_dynamic-update-slice_fusion.2
  732.4 96.1 %psum.7 = f32[30]{0:T(128)S(1)} all-reduce(f32[30]{0:T(128)S(1)} %get-tuple-element.185), channel_id=1, replica_groups=mesh['row'=32,'col'=16] {'row','col'}, use_global_device_ids=true, to_apply=%region_11.12 | all-reduce | flops 30 | bytes 240 | tf_op jit(solution)/shard_map/psum | solution.py:97
  831.1 6.3 fusion.49
  837.8 20.4 %all_to_all.33 = f32[3,1,256,128]{3,1,0,2:T(1,128)S(1)} all-to-all(f32[3,1,256,128]{3,1,0,2:T(1,128)S(1)} %copy.26), channel_id=1, replica_groups=mesh['row'=32,'col'=16] {'row'}, dimensions={2} | all-to-all | bytes 786432 | tf_op jit(solution)/shard_map/all_to_all | solution.py:111
  (335 shorter events, 276.0 us)
Async XLA Ops:
  0.6 23.7 %copy-start.2 = (s32[30]{0:T(128)S(1)}, s32[30]{0:T(128)}, u32[]{:S(2)}) copy-start(s32[30]{0:T(128)} %param.10) | copy-start | bytes 364
  0.6 23.7 %copy-start.3 = (f32[10]{0:T(128)S(1)}, f32[10]{0:T(128)}, u32[]{:S(2)}) copy-start(f32[10]{0:T(128)} %param.11) | copy-start | bytes 124
  0.6 6.6 collective-permute-start
  2.7 6.5 collective-permute-start.1
  11.1 272.8 %all-to-all-start.1 = ((bf16[3,32,8,128]{3,2,0,1:T(8,128)(2,1)}), bf16[3,32,8,128]{3,2,0,1:T(8,128)(2,1)S(1)}, u32[]{:S(2)}, u32[]{:S(2)}) async-start(bf16[3,32,8,128]{3,2,0,1:T(8,128)(2,1)} %slice.4), calls=%async_computation.1 | async-start | bytes 393216 | tf_op jit(solution)/shard_map/all_to_all | solution.py:81
  283.9 58.4 %all-to-all-start = ((bf16[30,32,8,128]{3,2,0,1:T(8,128)(2,1)}), bf16[30,32,8,128]{3,2,0,1:T(8,128)(2,1)S(1)}, u32[]{:S(2)}, u32[]{:S(2)}) async-start(bf16[30,32,8,128]{3,2,0,1:T(8,128)(2,1)} %get-tuple-element.184), calls=%async_computation | async-start | bytes 3932160 | tf_op jit(solution)/shard_map/all_to_all | solution.py:80
  829.1 8.3 copy-start.1
  831.1 27.2 %copy-start = (f32[32,8,128]{2,1,0:T(8,128)S(1)}, f32[32,8,128]{2,1,0:T(8,128)}, u32[]{:S(2)}) copy-start(f32[32,8,128]{2,1,0:T(8,128)} %param.8) | copy-start | bytes 393220
where the time goes:
time: 866 us; the launch traced here: 859 us
  loops' own time  293 us (34%)
  other arithmetic  219 us (25%)
  blocking collectives  116 us (13%)
  matrix products  89.1 us (10%)
  local copies, waits for them, and re-layouts  60.6 us (7%)
  waiting for transfers between devices  50.7 us (6%)
  starting transfers between devices  28.6 us (3%)
    another operation x1, loops' own time, per_device(): smoothed, partials = lax.map(along_y, channel_ids)  174 us
    another operation x1, loops' own time, per_device(): panels = lax.map(partial(smooth_x, wide), channel_ids)  119 us
    psum x1, blocking collectives, per_device(): compliance = lax.psum(partials, ('row', 'col')) / cell_count  96.1 us
    reduce_sum x60, other arithmetic, width_of(): jnp.sum(jnp.where(jnp.arange(channel_width.shape[0]) == index, channel_wi...  80.9 us
    reduce_sum x60, other arithmetic, width_of(): jnp.sum(jnp.where(jnp.arange(sigma_table.shape[0]) == slot, sigma_table,...  75.4 us
    dot_general x30, matrix products, along_y(): jnp.einsum('zyx,yw->zwx', source, matrix, preferred_element_type=jnp.floa...  54.6 us
    all_to_all x1, waiting for transfers between devices, per_device(): lax.all_to_all(panels, 'row', split_axis=1, concat_axis=2, tiled=True)  48.5 us
    reduce_sum x60, other arithmetic, gauss_band(): jnp.sum(jnp.exp(-tap_axis * tap_axis / (2.0 * width_value * width_value)))  39.1 us
  transfers between devices with their start and end apart: 4, of which 3 were waited for; matrix products, arithmetic and copies ran while one was open for 16% of the time, Pallas kernels for 0%

commit v1 on v0

--- a/solution.py
+++ b/solution.py
@@ -94,7 +94,7 @@
     cell_count = (
         lax.axis_size("row") * lax.axis_size("col") * variants.shape[1] * length * variants.shape[3]
     )
-    compliance = lax.psum(partials, ("row", "col")) / cell_count
+    compliance = jnp.sum(lax.all_gather(partials, ("row", "col")), axis=0) / cell_count
     mean_value = jnp.mean(compliance)
     spread = jnp.sqrt(jnp.mean((compliance - mean_value) ** 2) + spread_floor)
     weights = (1.0 + (compliance - mean_value) / spread) / CHANNELS

time: 866 us -> 867 us (level)
    unnamed x0 -> x1, blocking collectives: none -> 96.4 us
    psum x1 -> x0, blocking collectives: 96.1 us -> none  [per_device(): compliance = lax.psum(partials, ('row', 'col')) / cell_count]
where the time goes in v1:
time: 867 us; the launch traced here: 860 us
  loops' own time  293 us (34%)
  other arithmetic  219 us (25%)
  blocking collectives  117 us (13%)
  matrix products  89.1 us (10%)
  local copies, waits for them, and re-layouts  61.1 us (7%)
  waiting for transfers between devices  50.7 us (6%)
  starting transfers between devices  28.6 us (3%)
    another operation x1, loops' own time, per_device(): smoothed, partials = lax.map(along_y, channel_ids)  174 us
    another operation x1, loops' own time, per_device(): panels = lax.map(partial(smooth_x, wide), channel_ids)  119 us
    unnamed x1, blocking collectives  96.4 us
    reduce_sum x60, other arithmetic, width_of(): jnp.sum(jnp.where(jnp.arange(channel_width.shape[0]) == index, channel_wi...  80.9 us
    reduce_sum x60, other arithmetic, width_of(): jnp.sum(jnp.where(jnp.arange(sigma_table.shape[0]) == slot, sigma_table,...  75.4 us
    dot_general x30, matrix products, along_y(): jnp.einsum('zyx,yw->zwx', source, matrix, preferred_element_type=jnp.floa...  54.6 us
    all_to_all x1, waiting for transfers between devices, per_device(): lax.all_to_all(panels, 'row', split_axis=1, concat_axis=2, tiled=True)  48.5 us
    reduce_sum x60, other arithmetic, gauss_band(): jnp.sum(jnp.exp(-tap_axis * tap_axis / (2.0 * width_value * width_value)))  39.1 us
  transfers between devices with their start and end apart: 4, of which 3 were waited for; matrix products, arithmetic and copies ran while one was open for 16% of the time, Pallas kernels for 0%

profile of v1, /device:TPU:16, one launch (start us, length us, event | category | flops | bytes accessed | tf_op | source)
XLA Modules:
  0.0 860.0 jit_solution(5085560956758222623)
XLA Ops:
  0.6 2.1 collective-permute-start
  2.7 3.6 collective-permute-start.1
  7.3 1.9 collective-permute-done.1
  11.1 13.2 %all-to-all-start.1 = ((bf16[3,32,8,128]{3,2,0,1:T(8,128)(2,1)}), bf16[3,32,8,128]{3,2,0,1:T(8,128)(2,1)S(1)}, u32[]{:S(2)}, u32[]{:S(2)}) async-start(bf16[3,32,8,128]{3,2,0,1:T(8,128)(2,1)} %slice.4), calls=%async_computation.1 | async-start | bytes 393216 | tf_op jit(solution)/shard_map/all_to_all | solution.py:81
  24.3 259.6 %while.26 = (s32[]{:T(128)}, bf16[30,32,8,128]{3,2,0,1:T(8,128)(2,1)}, s32[30]{0:T(128)S(1)}, bf16[3,32,8,384]{3,2,0,1:T(8,128)(2,1)S(1)}, s32[30]{0:T(128)S(1)}...) while((s32[]{:T(128)}, ...), condition=%wide.region_4.5_spmd, body=%wide.region_0.4_spmd.sunk | while | flops 25691788 | bytes 263137 | solution.py:77
  283.9 9.8 %all-to-all-start = ((bf16[30,32,8,128]{3,2,0,1:T(8,128)(2,1)}), bf16[30,32,8,128]{3,2,0,1:T(8,128)(2,1)S(1)}, u32[]{:S(2)}, u32[]{:S(2)}) async-start(bf16[30,32,8,128]{3,2,0,1:T(8,128)(2,1)} %get-tuple-element.184), calls=%async_computation | async-start | bytes 3932160 | tf_op jit(solution)/shard_map/all_to_all | solution.py:80
  293.8 48.5 %all-to-all-done = bf16[30,32,8,128]{3,2,0,1:T(8,128)(2,1)S(1)} async-done(((bf16[30,32,8,128]{3,2,0,1:T(8,128)(2,1)}), bf16[30,32,8,128]{3,2,0,1:T(8,128)(2,1)S(1)}, u32[]{:S(2)}, u32[]{:S(2)}) %all-to-all-start) | async-done | bytes 1966112 | tf_op jit(solution)/shard_map/all_to_all | solution.py:80
  342.3 1.8 copy.41
  344.2 388.2 %while.27 = (s32[]{:T(128)}, f32[30,1,256,128]{3,2,1,0:T(8,128)}, f32[30]{0:T(128)S(1)}, s32[30]{0:T(128)S(1)}, s32[30]{0:T(128)S(1)}, /*index=5*/f32[10]{0:T(12...) while((s32[]{:T(128)}, f32[30,1,256,128]{3,2,1,0:T(8,128)}, ...), condition=%wide.region_10.11_spmd, body=%wide.region_5.10_spmd.sunk | while | flops 17467012 | bytes 525359 | solution.py:93
  346.7 1.4 fusion.78
  351.9 1.8 bitcast_dynamic-update-slice_fusion.2
  359.6 1.4 fusion.78
  364.9 1.8 bitcast_dynamic-update-slice_fusion.2
  372.6 1.4 fusion.78
  377.8 1.8 bitcast_dynamic-update-slice_fusion.2
  385.5 1.4 fusion.78
  390.7 1.8 bitcast_dynamic-update-slice_fusion.2
  398.5 1.4 fusion.78
  403.7 1.8 bitcast_dynamic-update-slice_fusion.2
  411.4 1.4 fusion.78
  416.6 1.8 bitcast_dynamic-update-slice_fusion.2
  424.3 1.4 fusion.78
  429.6 1.8 bitcast_dynamic-update-slice_fusion.2
  437.3 1.4 fusion.78
  442.5 1.8 bitcast_dynamic-update-slice_fusion.2
  450.2 1.4 fusion.78
  455.5 1.8 bitcast_dynamic-update-slice_fusion.2
  463.2 1.4 fusion.78
  468.4 1.8 bitcast_dynamic-update-slice_fusion.2
  476.1 1.4 fusion.78
  481.3 1.8 bitcast_dynamic-update-slice_fusion.2
  489.1 1.4 fusion.78
  494.3 1.8 bitcast_dynamic-update-slice_fusion.2
  502.0 1.4 fusion.78
  507.2 1.8 bitcast_dynamic-update-slice_fusion.2
  514.9 1.4 fusion.78
  520.2 1.8 bitcast_dynamic-update-slice_fusion.2
  527.9 1.4 fusion.78
  533.1 1.8 bitcast_dynamic-update-slice_fusion.2
  546.0 1.8 bitcast_dynamic-update-slice_fusion.2
  559.0 1.8 bitcast_dynamic-update-slice_fusion.2
  566.7 1.4 fusion.78
  571.9 1.8 bitcast_dynamic-update-slice_fusion.2
  579.6 1.4 fusion.78
  584.9 1.8 bitcast_dynamic-update-slice_fusion.2
  597.8 1.8 bitcast_dynamic-update-slice_fusion.2
  605.5 1.4 fusion.78
  610.8 1.8 bitcast_dynamic-update-slice_fusion.2
  623.7 1.8 bitcast_dynamic-update-slice_fusion.2
  636.6 1.8 bitcast_dynamic-update-slice_fusion.2
  644.3 1.4 fusion.78
  649.6 1.8 bitcast_dynamic-update-slice_fusion.2
  657.3 1.4 fusion.78
  662.5 1.8 bitcast_dynamic-update-slice_fusion.2
  675.5 1.8 bitcast_dynamic-update-slice_fusion.2
  688.4 1.8 bitcast_dynamic-update-slice_fusion.2
  696.1 1.4 fusion.78
  701.4 1.8 bitcast_dynamic-update-slice_fusion.2
  709.1 1.4 fusion.78
  714.3 1.8 bitcast_dynamic-update-slice_fusion.2
  727.2 1.8 bitcast_dynamic-update-slice_fusion.2
  732.7 96.4 %all-reduce = f32[15360]{0:T(1024)S(1)} all-reduce(f32[15360]{0:T(1024)S(1)} %dynamic-update-slice), channel_id=2, replica_groups=mesh['row'=32,'col'=16] {'row','col'}, use_global_device_ids=true, to_apply=%add | all-reduce | flops 15360 | bytes 122880
  832.0 6.3 fusion.49
  838.7 20.5 %all_to_all.33 = f32[3,1,256,128]{3,1,0,2:T(1,128)S(1)} all-to-all(f32[3,1,256,128]{3,1,0,2:T(1,128)S(1)} %copy.27), channel_id=1, replica_groups=mesh['row'=32,'col'=16] {'row'}, dimensions={2} | all-to-all | bytes 786432 | tf_op jit(solution)/shard_map/all_to_all | solution.py:111
  (339 shorter events, 276.6 us)
Async XLA Ops:
  0.6 23.7 %copy-start.2 = (s32[30]{0:T(128)S(1)}, s32[30]{0:T(128)}, u32[]{:S(2)}) copy-start(s32[30]{0:T(128)} %param.10) | copy-start | bytes 364
  0.6 23.7 %copy-start.3 = (f32[10]{0:T(128)S(1)}, f32[10]{0:T(128)}, u32[]{:S(2)}) copy-start(f32[10]{0:T(128)} %param.11) | copy-start | bytes 124
  0.6 6.6 collective-permute-start
  2.7 6.5 collective-permute-start.1
  11.1 272.8 %all-to-all-start.1 = ((bf16[3,32,8,128]{3,2,0,1:T(8,128)(2,1)}), bf16[3,32,8,128]{3,2,0,1:T(8,128)(2,1)S(1)}, u32[]{:S(2)}, u32[]{:S(2)}) async-start(bf16[3,32,8,128]{3,2,0,1:T(8,128)(2,1)} %slice.4), calls=%async_computation.1 | async-start | bytes 393216 | tf_op jit(solution)/shard_map/all_to_all | solution.py:81
  283.9 58.4 %all-to-all-start = ((bf16[30,32,8,128]{3,2,0,1:T(8,128)(2,1)}), bf16[30,32,8,128]{3,2,0,1:T(8,128)(2,1)S(1)}, u32[]{:S(2)}, u32[]{:S(2)}) async-start(bf16[30,32,8,128]{3,2,0,1:T(8,128)(2,1)} %get-tuple-element.184), calls=%async_computation | async-start | bytes 3932160 | tf_op jit(solution)/shard_map/all_to_all | solution.py:80
  830.0 8.3 copy-start.1
  832.0 27.2 %copy-start = (f32[32,8,128]{2,1,0:T(8,128)S(1)}, f32[32,8,128]{2,1,0:T(8,128)}, u32[]{:S(2)}) copy-start(f32[32,8,128]{2,1,0:T(8,128)} %param.8) | copy-start | bytes 393220
